TPU v7x, 256 devices: a whole 4x4x8 slice. The times are simulated.
256 devices in a mesh: row: 32 (over z_hi, x, core), col: 8 (over y, z_lo).
Axes of the slice: x: 4, y: 4, z: 8 (z_hi: 4, z_lo: 2; z = z_hi * 2 + z_lo), core: 2. Of those that a mesh axis runs over, the one named last changes fastest.
Arguments:
- row_features: bfloat16 [512, 256], P(('row', 'col')), may hold values from -6 to 6
- col_features: bfloat16 [2048, 256], P(('col', 'row')), may hold values from -6 to 6
- row_proj: bfloat16 [256, 64], replicated, may hold values from -0.375 to 0.375
- col_proj: bfloat16 [256, 64], replicated, may hold values from -0.375 to 0.375
- pair_weight: bfloat16 [2, 3, 3, 64, 64], replicated, may hold values from -0.1875 to 0.1875
- pair_bias: float32 [64], replicated, may hold values from -4 to 4
- conv_weight: bfloat16 [3, 3, 64, 64], replicated, may hold values from -0.25 to 0.25
- dilations: int32 [2], replicated, may hold values from 1 to 8, as said below
- cotangent: bfloat16 [64, 512, 2048], P(None, 'row', 'col'), may hold values from -6 to 6
Outputs:
- pair_out: bfloat16 [64, 512, 2048], P(None, 'row', 'col')
- grad_row_features: float32 [512, 256], P(('row', 'col'))
- grad_col_features: float32 [2048, 256], P(('col', 'row'))
- grad_row_proj: float32 [256, 64], replicated
- grad_col_proj: float32 [256, 64], replicated
- grad_pair_weight: float32 [2, 3, 3, 64, 64], replicated
- grad_pair_bias: float32 [64], replicated
- grad_conv_weight: float32 [3, 3, 64, 64], replicated
Inputs may be any that keep to these rules, and one draw needn't show every extreme that they name: One of the two dilations equals 8.
All inputs are finite; a program needn't handle non-finite values.
Results may differ from a plain program's by a relative error of at most 0.0054.
Values may be sent and summed in bfloat16 or wider, within the bound.
A program may use at most 64 MiB of HBM per device.

v0:
```python
import jax
import jax.numpy as jnp
from jax import lax
from jax.sharding import PartitionSpec as P

MAX_DILATION = 8


def sent_to_all(value, axis):
    copies = jnp.broadcast_to(value, (lax.axis_size(axis), *value.shape))
    return lax.all_to_all(copies, axis, split_axis=0, concat_axis=0, tiled=True)


def in_order(tiles, dim):
    dims = list(tiles.shape[1:])
    dims[dim] *= tiles.shape[0]
    return jnp.moveaxis(tiles, 0, dim).reshape(dims)


def gathered_copies(value, axis, dim):
    tiles = sent_to_all(value, axis)
    return in_order(tiles, dim)


def padded_2(value, sides, width):
    for axis, dim in sides:
        devices, length = (lax.axis_size(axis), value.shape[dim])
        up = [(i, (i + 1) % devices) for i in range(devices - 1)]
        down = [(j, i) for i, j in up]
        last = lax.slice_in_dim(value, length - width, length, axis=dim)
        leading = lax.slice_in_dim(value, 0, width, axis=dim)
        before = lax.ppermute(last, axis, up)
        after = lax.ppermute(leading, axis, down)
        value = jnp.concatenate([before, value, after], axis=dim)
    return value


def over_copies(value, axis):
    everything = sent_to_all(value, axis)
    return jnp.sum(everything, axis=0)


def total_of_pieces(value, axis):
    tiles = lax.all_gather(value, axis)
    return tiles.sum(axis=0)


def project(features, weight):
    return jnp.dot(features, weight, preferred_element_type=jnp.float32).astype(jnp.bfloat16)


def line_terms(padded, weights, dilation, count, offset):
    shifted = jnp.stack(
        [
            lax.dynamic_slice_in_dim(padded, offset + (tap_idx - 1) * dilation, count, 0)
            for tap_idx in range(3)
        ]
    )
    return jnp.einsum("kip,kqpo->qio", shifted, weights, preferred_element_type=jnp.float32)


def line_valid(first_cell, count, cell_limit, dilation):
    cells = first_cell + jnp.arange(count, dtype=jnp.int32)
    columns = [
        (cells + (tap_idx - 1) * dilation >= 0) & (cells + (tap_idx - 1) * dilation < cell_limit)
        for tap_idx in range(3)
    ]
    return jnp.stack(columns, axis=1).astype(jnp.float32)


def inside_mask(first_cell, count, cell_limit):
    cells = first_cell + jnp.arange(count, dtype=jnp.int32)
    return ((cells >= 0) & (cells < cell_limit)).astype(jnp.float32)


def pair_field(row_terms, col_terms, row_valid, col_valid, bias):
    from_rows = jnp.einsum("jq,qic->cij", col_valid, row_terms, precision=lax.Precision.HIGHEST)
    from_cols = jnp.einsum("ik,kjc->cij", row_valid, col_terms, precision=lax.Precision.HIGHEST)
    return from_rows + from_cols + bias[:, None, None]


def window_at(padded, row_index, col_index, rows, cols):
    anchor = jnp.zeros((), jnp.int32)
    return lax.dynamic_slice(padded, (anchor, row_index, col_index), (padded.shape[0], rows, cols))


def conv_taps(padded, weight, dilation, rows, cols, margin):
    result = jnp.zeros((weight.shape[3], rows, cols), jnp.float32)
    for tap_row in range(3):
        for tap_col in range(3):
            window = window_at(
                padded,
                margin + (tap_row - 1) * dilation,
                margin + (tap_col - 1) * dilation,
                rows,
                cols,
            )
            result = result + jnp.einsum(
                "co,cij->oij", weight[tap_row, tap_col], window, preferred_element_type=jnp.float32
            )
    return result


def back_taps(padded, weight, dilation, rows, cols, margin):
    result = jnp.zeros((weight.shape[2], rows, cols), jnp.float32)
    for tap_row in range(3):
        for tap_col in range(3):
            window = window_at(
                padded,
                margin - (tap_row - 1) * dilation,
                margin - (tap_col - 1) * dilation,
                rows,
                cols,
            )
            result = result + jnp.einsum(
                "co,oij->cij", weight[tap_row, tap_col], window, preferred_element_type=jnp.float32
            )
    return result


def tap_grads(hidden_pad, grads, dilation, rows, cols, margin):
    stacked = []
    for tap_row in range(3):
        line_list = []
        for tap_col in range(3):
            window = window_at(
                hidden_pad,
                margin + (tap_row - 1) * dilation,
                margin + (tap_col - 1) * dilation,
                rows,
                cols,
            )
            line_list.append(
                jnp.einsum("cij,oij->co", window, grads, preferred_element_type=jnp.float32)
            )
        stacked.append(jnp.stack(line_list))
    return jnp.stack(stacked)


def shards(
    row_features,
    col_features,
    row_proj,
    col_proj,
    pair_weight,
    pair_bias,
    conv_weight,
    dilations,
    cotangent,
):
    first_rate = dilations[0]
    second_rate = dilations[1]
    margin = MAX_DILATION
    row_count = lax.axis_size("row")
    col_count = lax.axis_size("col")
    row_place = lax.axis_index("row")
    col_place = lax.axis_index("col")
    rows_here = cotangent.shape[1]
    cols_here = cotangent.shape[2]
    row_start = row_place * rows_here
    col_start = col_place * cols_here
    row_limit = rows_here * row_count
    col_limit = cols_here * col_count
    row_piece = row_features.shape[0]
    col_piece = col_features.shape[0]
    rows_a = gathered_copies(project(row_features, row_proj), "col", 0)
    cols_b = gathered_copies(project(col_features, col_proj), "row", 0)
    pad_reach = 2 * margin
    a_pad = padded_2(rows_a, (("row", 0),), 2 * MAX_DILATION)
    b_pad = padded_2(cols_b, (("col", 0),), 2 * MAX_DILATION)
    row_terms = line_terms(
        a_pad, pair_weight[0], first_rate, rows_here + 2 * margin, pad_reach - margin
    )
    col_terms = line_terms(
        b_pad,
        jnp.swapaxes(pair_weight[1], 0, 1),
        first_rate,
        cols_here + 2 * margin,
        pad_reach - margin,
    )
    row_valid = line_valid(row_start - margin, rows_here + 2 * margin, row_limit, first_rate)
    col_valid = line_valid(col_start - margin, cols_here + 2 * margin, col_limit, first_rate)
    pre_act = pair_field(row_terms, col_terms, row_valid, col_valid, pair_bias)
    row_inside = inside_mask(row_start - margin, rows_here + 2 * margin, row_limit)
    col_inside = inside_mask(col_start - margin, cols_here + 2 * margin, col_limit)
    hidden = (jax.nn.silu(pre_act) * row_inside[None, :, None] * col_inside[None, None, :]).astype(
        jnp.bfloat16
    )
    pre_own = pre_act[:, margin : margin + rows_here, margin : margin + cols_here]
    hidden_own = hidden[:, margin : margin + rows_here, margin : margin + cols_here]
    conv_mixed = conv_taps(hidden, conv_weight, second_rate, rows_here, cols_here, margin)
    pair_out = (hidden_own.astype(jnp.float32) + conv_mixed).astype(jnp.bfloat16)
    grad_pad = padded_2(cotangent, (("row", 1), ("col", 2)), MAX_DILATION)
    d_hidden = cotangent.astype(jnp.float32) + back_taps(
        grad_pad, conv_weight, second_rate, rows_here, cols_here, margin
    )
    conv_grad = tap_grads(hidden, cotangent, second_rate, rows_here, cols_here, margin)
    sigmoid_own = jax.nn.sigmoid(pre_own)
    d_pre = d_hidden * sigmoid_own * (1.0 + pre_own * (1.0 - sigmoid_own))
    bias_grad = jnp.sum(d_pre, axis=(1, 2))
    row_valid_own = line_valid(row_start, rows_here, row_limit, first_rate)
    col_valid_own = line_valid(col_start, cols_here, col_limit, first_rate)
    row_part = jnp.einsum("jq,cij->qic", col_valid_own, d_pre, precision=lax.Precision.HIGHEST)
    col_part = jnp.einsum("ik,cij->kjc", row_valid_own, d_pre, precision=lax.Precision.HIGHEST)
    row_sums = over_copies(row_part, "col")
    col_sums = total_of_pieces(col_part, "row")
    back_rows = jnp.einsum(
        "qio,kqpo->kip",
        row_sums,
        pair_weight[0].astype(jnp.float32),
        precision=lax.Precision.HIGHEST,
    )
    back_cols = jnp.einsum(
        "kjo,kqpo->qjp",
        col_sums,
        pair_weight[1].astype(jnp.float32),
        precision=lax.Precision.HIGHEST,
    )
    rows_back_pad = padded_2(back_rows, (("row", 1),), MAX_DILATION)
    cols_back_pad = padded_2(back_cols, (("col", 1),), MAX_DILATION)
    row_own = col_place * row_piece
    col_own = row_place * col_piece
    d_rows = sum(
        (
            lax.dynamic_slice_in_dim(
                rows_back_pad[tap_idx], margin + row_own - (tap_idx - 1) * first_rate, row_piece, 0
            )
            for tap_idx in range(3)
        )
    )
    d_cols = sum(
        (
            lax.dynamic_slice_in_dim(
                cols_back_pad[tap_idx], margin + col_own - (tap_idx - 1) * first_rate, col_piece, 0
            )
            for tap_idx in range(3)
        )
    )
    d_rows = d_rows.astype(jnp.bfloat16)
    d_cols = d_cols.astype(jnp.bfloat16)
    grad_row_features = jnp.dot(d_rows, row_proj.T, preferred_element_type=jnp.float32)
    grad_col_features = jnp.dot(d_cols, col_proj.T, preferred_element_type=jnp.float32)
    grad_row_proj = jnp.dot(row_features.T, d_rows, preferred_element_type=jnp.float32)
    grad_col_proj = jnp.dot(col_features.T, d_cols, preferred_element_type=jnp.float32)
    row_shifted = jnp.stack(
        [
            lax.dynamic_slice_in_dim(
                a_pad, pad_reach + row_own + (tap_idx - 1) * first_rate, row_piece, 0
            )
            for tap_idx in range(3)
        ]
    )
    col_shifted = jnp.stack(
        [
            lax.dynamic_slice_in_dim(
                b_pad, pad_reach + col_own + (tap_idx - 1) * first_rate, col_piece, 0
            )
            for tap_idx in range(3)
        ]
    )
    row_sums_own = lax.dynamic_slice_in_dim(row_sums, row_own, row_piece, 1)
    col_sums_own = lax.dynamic_slice_in_dim(col_sums, col_own, col_piece, 1)
    grad_row_pair = jnp.einsum(
        "kip,qio->kqpo",
        row_shifted.astype(jnp.float32),
        row_sums_own,
        precision=lax.Precision.HIGHEST,
    )
    grad_col_pair = jnp.einsum(
        "qjp,kjo->kqpo",
        col_shifted.astype(jnp.float32),
        col_sums_own,
        precision=lax.Precision.HIGHEST,
    )
    summed = lax.psum(
        (
            grad_row_proj,
            grad_col_proj,
            jnp.stack([grad_row_pair, grad_col_pair]),
            bias_grad,
            conv_grad,
        ),
        ("row", "col"),
    )
    return (
        pair_out,
        grad_row_features,
        grad_col_features,
        summed[0],
        summed[1],
        summed[2],
        summed[3],
        summed[4],
    )


def solution(mesh):
    return jax.shard_map(
        shards,
        mesh=mesh,
        in_specs=(
            P(("row", "col"), None),
            P(("col", "row"), None),
            P(),
            P(),
            P(),
            P(),
            P(),
            P(),
            P(None, "row", "col"),
        ),
        out_specs=(
            P(None, "row", "col"),
            P(("row", "col"), None),
            P(("col", "row"), None),
            P(),
            P(),
            P(),
            P(),
            P(),
        ),
        check_vma=False,
    )
```

profile of v0, /device:TPU:8, one launch (start us, length us, event | category | flops | bytes accessed | tf_op | source)
XLA Modules:
  0.0 497.2 jit_solution(1693750690878822578)
XLA Ops:
  7.2 1.0 convolution_convert_fusion.1
  8.2 0.6 broadcast_in_dim.12
  8.8 6.3 %all-to-all-start = ((bf16[8,2,64]{2,1,0:T(2,128)(2,1)}), bf16[8,2,64]{2,1,0:T(2,128)(2,1)S(1)}, u32[]{:S(2)}, u32[]{:S(2)}) async-start(bf16[8,2,64]{2,1,0:T(2,128)(2,1)} %broadcast_in_dim.12), calls=%async_computation | async-start | bytes 8192 | tf_op jit(solution)/shard_map/all_to_all | solution.py:11
  15.1 1.1 fusion.201
  16.2 1.3 collective-permute-start.4
  17.6 1.3 collective-permute-start.5
  18.9 0.6 fusion.207
  20.1 0.7 compare_and_fusion.9
  20.8 1.2 compare_and_fusion
  22.0 0.5 and_convert_fusion
  22.6 0.7 compare_and_fusion.6
  23.3 1.0 fusion.73
  24.4 0.6 compare_and_fusion.8
  25.0 0.7 reshape.293
  25.7 15.1 %all-to-all-start.1 = ((bf16[32,2,256]{2,1,0:T(2,128)(2,1)}), bf16[32,2,256]{2,1,0:T(2,128)(2,1)S(1)}, u32[]{:S(2)}, u32[]{:S(2)}) async-start(bf16[32,2,256]{2,1,0:T(2,128)(2,1)} %reshape.293), calls=%async_computation.1 | async-start | bytes 65536 | tf_op jit(solution)/shard_map/all_to_all | solution.py:11
  40.9 2.2 collective-permute-start
  43.1 1.3 collective-permute-start.1
  49.2 1.5 all-to-all-done.1
  51.0 3.3 collective-permute-start.2
  54.4 3.4 collective-permute-start.3
  57.8 0.8 convolution_bitcast_fusion.11
  58.7 1.3 collective-permute-done.3
  60.5 1.5 fusion.46
  62.6 4.3 collective-permute-start.6
  66.9 2.6 collective-permute-start.7
  69.5 4.6 multiply_convert_fusion
  74.2 6.0 %collective-permute-done.6 = bf16[64,32,8]{2,0,1:T(8,128)(2,1)S(1)} collective-permute-done((bf16[64,32,8]{2,0,1:T(8,128)(2,1)S(1)}, bf16[64,32,8]{2,0,1:T(8,128)(2,1)S(1)}, u32[]{:S(2)}, u32[]{:S(2)}) %collective-permute-start.6) | collective-permute-done | bytes 32800 | tf_op jit(solution)/shard_map/ppermute | solution.py:32
  80.2 9.6 %collective-permute-done.7 = bf16[64,32,8]{2,0,1:T(8,128)(2,1)S(1)} collective-permute-done((bf16[64,32,8]{2,0,1:T(8,128)(2,1)S(1)}, bf16[64,32,8]{2,0,1:T(8,128)(2,1)S(1)}, u32[]{:S(2)}, u32[]{:S(2)}) %collective-permute-start.7) | collective-permute-done | bytes 32800 | tf_op jit(solution)/shard_map/ppermute | solution.py:33
  89.8 1.1 pad_maximum_fusion
  93.1 0.5 fusion.11
  93.7 1.8 fusion.208
  95.4 1.1 convolution_bitcast_fusion.7
  96.5 0.7 copy.231
  101.8 0.7 compare_and_fusion.3
  102.5 0.5 fusion.174
  104.4 0.6 maximum_bitcast_fusion.2
  105.5 0.7 convolution_bitcast_fusion.12
  106.6 0.7 maximum_bitcast_fusion.4
  107.7 1.1 convolution_bitcast_fusion.15
  109.2 1.1 convolution_bitcast_fusion.16
  113.6 0.7 convolution_bitcast_fusion.21
  114.3 0.8 reshape.295
  115.2 4.9 all-to-all-start.2
  120.2 0.7 pad_maximum_fusion.3
  120.9 4.6 all-to-all-done.2
  126.0 0.9 reduce
  127.3 1.3 collective-permute-start.8
  128.6 1.3 collective-permute-start.9
  130.2 1.1 copy.246
  131.3 81.3 %psum.38 = f32[64]{0:T(128)} all-reduce(f32[64]{0:T(128)S(1)} %copy-done.22), channel_id=1, replica_groups=mesh['row'=32,'col'=8] {'row','col'}, use_global_device_ids=true, to_apply=%region_6.7 | all-reduce | flops 64 | bytes 512 | tf_op jit(solution)/shard_map/psum | solution.py:275
  213.1 0.8 convolution_bitcast_fusion.10
  213.9 3.2 reduce_sum.28
  217.5 3.2 collective-permute-start.10
  220.7 3.5 collective-permute-start.11
  224.6 0.9 pad_maximum_fusion.1
  225.5 1.8 collective-permute-done.11
  227.6 0.8 convolution_bitcast_fusion.9
  228.3 0.7 fusion.178
  229.1 0.8 fusion.211
  229.8 254.7 %all-reduce.3.cloned.1.call-done = (f32[256,64]{0,1:T(8,128)}, f32[256,64]{0,1:T(8,128)}, f32[2,3,3,64,64]{3,4,1,2,0:T(8,128)}, f32[3,3,64,64]{3,2,1,0:T(8,128)}) async-done(((f32[256,64]{0,1:T(8,128)}, f32[256,64]{0,1:T(8,128)}, f32[2,3,3,64,64]{3,4,1,2,0:T(8,128)}, f32[3,3,64,64]{3,2,1,0:T(8,128)}), (f32[256,64]{0,1:T(8,128)}, f32[256,64]{0,1:T(8,128)}, f32[2,3,3,64,64]{3,4,1,2,0:T(8,128)}, ...) | async-done | bytes 573456 | tf_op jit(solution)/shard_map/psum | solution.py:275
  484.5 2.1 copy.247
  486.7 1.5 copy.329
  488.2 1.5 copy.330
  489.6 0.7 copy.331
  (128 shorter events, 13.2 us)
Async XLA Ops:
  7.2 17.1 %copy-start = (bf16[256,64]{0,1:T(8,128)(2,1)S(1)}, bf16[256,64]{0,1:T(8,128)(2,1)}, u32[]{:S(2)}) copy-start(bf16[256,64]{0,1:T(8,128)(2,1)} %param.12) | copy-start | bytes 98308
  7.2 16.1 %copy-start.1 = (bf16[64,16,256]{2,1,0:T(8,128)(2,1)S(1)}, bf16[64,16,256]{2,1,0:T(8,128)(2,1)}, u32[]{:S(2)}) copy-start(bf16[64,16,256]{2,1,0:T(8,128)(2,1)} %param.17) | copy-start | bytes 1572868
  7.2 11.7 %copy-start.16 = (s32[2]{0:T(128)S(1)}, s32[2]{0:T(128)}, u32[]{:S(2)}) copy-start(s32[2]{0:T(128)} %param.16) | copy-start | bytes 28
  7.2 16.0 %copy-start.2 = (bf16[2,3,3,64,64]{4,3,2,1,0:T(8,128)(2,1)S(1)}, bf16[2,3,3,64,64]{4,3,2,1,0:T(8,128)(2,1)}, u32[]{:S(2)}) copy-start(bf16[2,3,3,64,64]{4,3,2,1,0:T(8,128)(2,1)} %param.13) | copy-start | bytes 442372
  8.8 16.9 %all-to-all-start = ((bf16[8,2,64]{2,1,0:T(2,128)(2,1)}), bf16[8,2,64]{2,1,0:T(2,128)(2,1)S(1)}, u32[]{:S(2)}, u32[]{:S(2)}) async-start(bf16[8,2,64]{2,1,0:T(2,128)(2,1)} %broadcast_in_dim.12), calls=%async_computation | async-start | bytes 8192 | tf_op jit(solution)/shard_map/all_to_all | solution.py:11
  16.1 8.2 %copy-start.11 = (bf16[8,256]{1,0:T(8,128)(2,1)S(1)}, bf16[8,256]{1,0:T(8,128)(2,1)}, u32[]{:S(2)}) copy-start(bf16[8,256]{1,0:T(8,128)(2,1)} %param.10) | copy-start | bytes 12292
  16.2 45.8 %collective-permute-start.4 = (bf16[64,8,256]{2,0,1:T(8,128)(2,1)S(1)}, bf16[64,8,256]{2,0,1:T(8,128)(2,1)S(1)}, u32[]{:S(2)}, u32[]{:S(2)}) collective-permute-start(bf16[64,8,256]{2,0,1:T(8,128)(2,1)S(1)} %copy.319), channel_id=1, source_target_pairs={{0,8},{8,16},{16,24},{24,32},{32,40},{40,48},{48,56},{56,64},{64,7... | collective-permute-start | bytes 786440 | tf_op jit(solution)/shard_map/ppermute | solution.py:32
  17.6 44.7 %collective-permute-start.5 = (bf16[64,8,256]{2,0,1:T(8,128)(2,1)S(1)}, bf16[64,8,256]{2,0,1:T(8,128)(2,1)S(1)}, u32[]{:S(2)}, u32[]{:S(2)}) collective-permute-start(bf16[64,8,256]{2,0,1:T(8,128)(2,1)S(1)} %copy.320), channel_id=1, source_target_pairs={{8,0},{16,8},{24,16},{32,24},{40,32},{48,40},{56,48},{64,56},{72,6... | collective-permute-start | bytes 786440 | tf_op jit(solution)/shard_map/ppermute | solution.py:33
  25.7 25.0 %all-to-all-start.1 = ((bf16[32,2,256]{2,1,0:T(2,128)(2,1)}), bf16[32,2,256]{2,1,0:T(2,128)(2,1)S(1)}, u32[]{:S(2)}, u32[]{:S(2)}) async-start(bf16[32,2,256]{2,1,0:T(2,128)(2,1)} %reshape.293), calls=%async_computation.1 | async-start | bytes 65536 | tf_op jit(solution)/shard_map/all_to_all | solution.py:11
  40.9 173.0 %all-gather.3.cloned.1.call-start = ((), (), s32[]{:S(2)}) async-start(), calls=%async_computation.3 | async-start | bytes 6488064 | tf_op jit(solution)/shard_map/all_gather | solution.py:44
  40.9 8.2 %collective-permute-start = (bf16[16,64]{1,0:T(8,128)(2,1)S(1)}, bf16[16,64]{1,0:T(8,128)(2,1)S(1)}, u32[]{:S(2)}, u32[]{:S(2)}) collective-permute-start(bf16[16,64]{1,0:T(8,128)(2,1)S(1)} %bitcast.322), channel_id=1, source_target_pairs={{0,8},{8,16},{16,24},{24,32},{32,40},{40,48},{48,56},{56,64},{64,7... | collective-permute-start | bytes 6152 | tf_op jit(solution)/shard_map/ppermute | solution.py:32
  43.1 6.0 %collective-permute-start.1 = (bf16[16,64]{1,0:T(8,128)(2,1)S(1)}, bf16[16,64]{1,0:T(8,128)(2,1)S(1)}, u32[]{:S(2)}, u32[]{:S(2)}) collective-permute-start(bf16[16,64]{1,0:T(8,128)(2,1)S(1)} %bitcast.323), channel_id=1, source_target_pairs={{8,0},{16,8},{24,16},{32,24},{40,32},{48,40},{56,48},{64,56},{72,6... | collective-permute-start | bytes 6152 | tf_op jit(solution)/shard_map/ppermute | solution.py:33
  51.0 7.8 %collective-permute-start.2 = (bf16[16,64]{0,1:T(8,128)(2,1)S(1)}, bf16[16,64]{0,1:T(8,128)(2,1)S(1)}, u32[]{:S(2)}, u32[]{:S(2)}) collective-permute-start(bf16[16,64]{0,1:T(8,128)(2,1)S(1)} %copy.199), channel_id=1, source_target_pairs={{0,1},{1,2},{2,3},{3,4},{4,5},{5,6},{6,7},{8,9},{9,10},{10,11},{11... | collective-permute-start | bytes 6152 | tf_op jit(solution)/shard_map/ppermute | solution.py:32
  54.4 5.6 %collective-permute-start.3 = (bf16[16,64]{0,1:T(8,128)(2,1)S(1)}, bf16[16,64]{0,1:T(8,128)(2,1)S(1)}, u32[]{:S(2)}, u32[]{:S(2)}) collective-permute-start(bf16[16,64]{0,1:T(8,128)(2,1)S(1)} %copy.200), channel_id=1, source_target_pairs={{1,0},{2,1},{3,2},{4,3},{5,4},{6,5},{7,6},{9,8},{10,9},{11,10},{12... | collective-permute-start | bytes 6152 | tf_op jit(solution)/shard_map/ppermute | solution.py:33
  62.2 7.3 %copy-start.17 = (pred[272,1]{0,1:T(4,128)(4,1)S(1)}, pred[272,1]{0,1:T(4,128)(4,1)}, u32[]{:S(2)}) copy-start(pred[272,1]{0,1:T(4,128)(4,1)} %get-tuple-element.89) | copy-start | bytes 820
  62.2 7.3 %copy-start.20 = (f32[64]{0:T(128)S(1)}, f32[64]{0:T(128)}, u32[]{:S(2)}) copy-start(f32[64]{0:T(128)} %param.14) | copy-start | bytes 772
  62.2 7.3 %copy-start.21 = (f32[3,32,64]{2,1,0:T(8,128)S(1)}, f32[3,32,64]{2,1,0:T(8,128)}, u32[]{:S(2)}) copy-start(f32[3,32,64]{2,1,0:T(8,128)} %convolution_bitcast_fusion.11) | copy-start | bytes 73732
  62.2 7.3 %copy-start.23 = (f32[32]{0:T(128)S(1)}, f32[32]{0:T(128)}, u32[]{:S(2)}) copy-start(f32[32]{0:T(128)} %and_convert_fusion) | copy-start | bytes 388
  62.6 17.7 %collective-permute-start.6 = (bf16[64,32,8]{2,0,1:T(8,128)(2,1)S(1)}, bf16[64,32,8]{2,0,1:T(8,128)(2,1)S(1)}, u32[]{:S(2)}, u32[]{:S(2)}) collective-permute-start(bf16[64,32,8]{2,0,1:T(8,128)(2,1)S(1)} %get-tuple-element.52), channel_id=1, source_target_pairs={{0,1},{1,2},{2,3},{3,4},{4,5},{5,6},{6,7},{8,9},{9,10},{10,11},{11... | collective-permute-start | bytes 98312 | tf_op jit(solution)/shard_map/ppermute | solution.py:32
  66.9 22.9 %collective-permute-start.7 = (bf16[64,32,8]{2,0,1:T(8,128)(2,1)S(1)}, bf16[64,32,8]{2,0,1:T(8,128)(2,1)S(1)}, u32[]{:S(2)}, u32[]{:S(2)}) collective-permute-start(bf16[64,32,8]{2,0,1:T(8,128)(2,1)S(1)} %get-tuple-element.53), channel_id=1, source_target_pairs={{1,0},{2,1},{3,2},{4,3},{5,4},{6,5},{7,6},{9,8},{10,9},{11,10},{12... | collective-permute-start | bytes 98312 | tf_op jit(solution)/shard_map/ppermute | solution.py:33
  74.2 16.7 %copy-start.3 = (bf16[3,3,64,64]{3,2,1,0:T(8,128)(2,1)S(1)}, bf16[3,3,64,64]{3,2,1,0:T(8,128)(2,1)}, u32[]{:S(2)}) copy-start(bf16[3,3,64,64]{3,2,1,0:T(8,128)(2,1)} %param.15) | copy-start | bytes 221188
  93.6 1.8 copy-start.19
  106.2 2.6 copy-start.4
  113.5 6.6 %copy-start.9 = (f32[1,64,64]{2,1,0:T(8,128)S(1)}, f32[1,64,64]{2,1,0:T(8,128)}, u32[]{:S(2)}) copy-start(f32[1,64,64]{2,1,0:T(8,128)} %convolution_bitcast_fusion.15) | copy-start | bytes 49156
  113.5 6.6 %copy-start.10 = (f32[1,64,64]{2,1,0:T(8,128)S(1)}, f32[1,64,64]{2,1,0:T(8,128)}, u32[]{:S(2)}) copy-start(f32[1,64,64]{2,1,0:T(8,128)} %convolution_bitcast_fusion.16) | copy-start | bytes 49156
  113.5 6.6 %copy-start.5 = (f32[1,3,64,64]{3,2,1,0:T(8,128)S(1)}, f32[1,3,64,64]{3,2,1,0:T(8,128)}, u32[]{:S(2)}) copy-start(f32[1,3,64,64]{3,2,1,0:T(8,128)} %maximum_bitcast_fusion.2) | copy-start | bytes 147460
  113.6 6.6 %copy-start.6 = (f32[1,3,64,64]{3,2,1,0:T(8,128)S(1)}, f32[1,3,64,64]{3,2,1,0:T(8,128)}, u32[]{:S(2)}) copy-start(f32[1,3,64,64]{3,2,1,0:T(8,128)} %maximum_bitcast_fusion.4) | copy-start | bytes 147460
  115.1 16.2 %copy-start.22 = (f32[64]{0:T(128)S(1)}, f32[64]{0:T(128)}, u32[]{:S(2)}) copy-start(f32[64]{0:T(128)} %get-tuple-element.86) | copy-start | bytes 772
  115.1 97.5 %copy-start.13 = (bf16[1,2,64]{2,1,0:T(2,128)(2,1)S(1)}, bf16[1,2,64]{2,1,0:T(2,128)(2,1)}, u32[]{:S(2)}) copy-start(bf16[1,2,64]{2,1,0:T(2,128)(2,1)} %get-tuple-element.76) | copy-start | bytes 772
  115.1 97.5 %copy-start.14 = (bf16[1,2,64]{2,1,0:T(2,128)(2,1)S(1)}, bf16[1,2,64]{2,1,0:T(2,128)(2,1)}, u32[]{:S(2)}) copy-start(bf16[1,2,64]{2,1,0:T(2,128)(2,1)} %get-tuple-element.77) | copy-start | bytes 772
  115.1 97.5 %copy-start.15 = (bf16[1,2,64]{2,1,0:T(2,128)(2,1)S(1)}, bf16[1,2,64]{2,1,0:T(2,128)(2,1)}, u32[]{:S(2)}) copy-start(bf16[1,2,64]{2,1,0:T(2,128)(2,1)} %get-tuple-element.78) | copy-start | bytes 772
  115.2 10.3 %all-to-all-start.2 = ((f32[8,1,3072]{2,1,0:T(1,128)}), f32[8,1,3072]{2,1,0:T(1,128)S(1)}, u32[]{:S(2)}, u32[]{:S(2)}) async-start(f32[8,1,3072]{2,1,0:T(1,128)} %reshape.295), calls=%async_computation.2 | async-start | bytes 196608 | tf_op jit(solution)/shard_map/all_to_all | solution.py:11
  120.1 364.5 %all-reduce.3.cloned.1.call-start = ((), (), s32[]{:S(2)}) async-start(), calls=%async_computation.4 | async-start | bytes 2031616 | tf_op jit(solution)/shard_map/psum | solution.py:275
  120.1 92.9 %copy-start.18 = (bf16[2,256]{1,0:T(2,128)(2,1)S(1)}, bf16[2,256]{1,0:T(2,128)(2,1)}, u32[]{:S(2)}) copy-start(bf16[2,256]{1,0:T(2,128)(2,1)} %param.9) | copy-start | bytes 3076
  127.3 85.7 %collective-permute-start.8 = (f32[3,8,64]{2,1,0:T(8,128)S(1)}, f32[3,8,64]{2,1,0:T(8,128)S(1)}, u32[]{:S(2)}, u32[]{:S(2)}) collective-permute-start(f32[3,8,64]{2,1,0:T(8,128)S(1)} %get-tuple-element.74), channel_id=1, source_target_pairs={{0,8},{8,16},{16,24},{24,32},{32,40},{40,48},{48,56},{56,64},{64,7... | collective-permute-start | bytes 18440 | tf_op jit(solution)/shard_map/ppermute | solution.py:32
  128.6 84.4 %collective-permute-start.9 = (f32[3,8,64]{2,1,0:T(8,128)S(1)}, f32[3,8,64]{2,1,0:T(8,128)S(1)}, u32[]{:S(2)}, u32[]{:S(2)}) collective-permute-start(f32[3,8,64]{2,1,0:T(8,128)S(1)} %get-tuple-element.75), channel_id=1, source_target_pairs={{8,0},{16,8},{24,16},{32,24},{40,32},{48,40},{56,48},{64,56},{72,6... | collective-permute-start | bytes 18440 | tf_op jit(solution)/shard_map/ppermute | solution.py:33
  217.5 10.1 %copy-start.12 = (bf16[8,256]{1,0:T(8,128)(2,1)S(1)}, bf16[8,256]{1,0:T(8,128)(2,1)}, u32[]{:S(2)}) copy-start(bf16[8,256]{1,0:T(8,128)(2,1)} %param.10) | copy-start | bytes 12292
  217.5 8.0 %collective-permute-start.10 = (f32[3,8,64]{1,2,0:T(8,128)S(1)}, f32[3,8,64]{1,2,0:T(8,128)S(1)}, u32[]{:S(2)}, u32[]{:S(2)}) collective-permute-start(f32[3,8,64]{1,2,0:T(8,128)S(1)} %get-tuple-element.61), channel_id=1, source_target_pairs={{0,1},{1,2},{2,3},{3,4},{4,5},{5,6},{6,7},{8,9},{9,10},{10,11},{11... | collective-permute-start | bytes 18440 | tf_op jit(solution)/shard_map/ppermute | solution.py:32
  220.7 6.5 %collective-permute-start.11 = (f32[3,8,64]{1,2,0:T(8,128)S(1)}, f32[3,8,64]{1,2,0:T(8,128)S(1)}, u32[]{:S(2)}, u32[]{:S(2)}) collective-permute-start(f32[3,8,64]{1,2,0:T(8,128)S(1)} %get-tuple-element.62), channel_id=1, source_target_pairs={{1,0},{2,1},{3,2},{4,3},{5,4},{6,5},{7,6},{9,8},{10,9},{11,10},{12... | collective-permute-start | bytes 18440 | tf_op jit(solution)/shard_map/ppermute | solution.py:33
  224.6 3.7 copy-start.8
  484.5 5.1 %copy-start.7 = (f32[3,3,64,64]{3,2,1,0:T(8,128)S(1)}, f32[3,3,64,64]{3,2,1,0:T(8,128)}, u32[]{:S(2)}) copy-start(f32[3,3,64,64]{3,2,1,0:T(8,128)} %get-tuple-element.103) | copy-start | bytes 442372
Sparse Core Ops, SparseCore 0:
  97.3 69.7 all-gather.2
  228.5 256.0 all-reduce.2
where the time goes:
time: 498 us; the launch traced here: 497 us
  waiting for transfers between devices  280 us (56%)
  blocking collectives  81.3 us (16%)
  starting transfers between devices  55.4 us (11%)
  matrix products  29 us (6%)
  between operations  24.8 us (5%)
  local copies, waits for them, and re-layouts  14.5 us (3%)
  other arithmetic  12.7 us (3%)
    psum x1, waiting for transfers between devices, shards(): lax.psum((grad_row_proj, grad_col_proj, jnp.stack([grad_row_pair, grad_co...  255 us
    psum x1, blocking collectives, shards(): lax.psum((grad_row_proj, grad_col_proj, jnp.stack([grad_row_pair, grad_co...  81.3 us
    all_to_all x3, starting transfers between devices, sent_to_all(): return lax.all_to_all(copies, axis, split_axis=0, concat_axis=0, tiled=True)  26.3 us
    ppermute x6, starting transfers between devices, padded_2(): before = lax.ppermute(last, axis, up)  15.6 us
    ppermute x6, starting transfers between devices, padded_2(): after = lax.ppermute(leading, axis, down)  13.4 us
    ppermute x6, waiting for transfers between devices, padded_2(): after = lax.ppermute(leading, axis, down)  12.6 us
  transfers between devices with their start and end apart: 17, of which 7 were waited for; matrix products, arithmetic and copies ran while one was open for 7% of the time, Pallas kernels for 0%

commit v1 on v0

--- a/solution.py
+++ b/solution.py
@@ -273,14 +273,17 @@
         precision=lax.Precision.HIGHEST,
     )
     summed = lax.psum(
-        (
-            grad_row_proj,
-            grad_col_proj,
-            jnp.stack([grad_row_pair, grad_col_pair]),
-            bias_grad,
-            conv_grad,
+        lax.psum(
+            (
+                grad_row_proj,
+                grad_col_proj,
+                jnp.stack([grad_row_pair, grad_col_pair]),
+                bias_grad,
+                conv_grad,
+            ),
+            axis_name="col",
         ),
-        ("row", "col"),
+        axis_name="row",
     )
     return (
         pair_out,

time: 498 us -> 570 us (1.14)
  waiting for transfers between devices: 280 us -> 341 us
  blocking collectives: 81.3 us -> 87.5 us
    psum x0 -> x1, waiting for transfers between devices: none -> 199 us  [shards(): lax.psum(lax.psum((grad_row_proj, grad_col_proj, jnp.stack([grad_row_pair...]
    psum x1, waiting for transfers between devices: 255 us -> 79.8 us  [shards(): lax.psum((grad_row_proj, grad_col_proj, jnp.stack([grad_row_pair, grad_co...]
    psum x0 -> x1, blocking collectives: none -> 70.4 us  [shards(): lax.psum(lax.psum((grad_row_proj, grad_col_proj, jnp.stack([grad_row_pair...]
    psum x1, blocking collectives: 81.3 us -> 17.1 us  [shards(): lax.psum((grad_row_proj, grad_col_proj, jnp.stack([grad_row_pair, grad_co...]
    all_gather x1, waiting for transfers between devices: 0.01 us -> 34 us  [total_of_pieces(): tiles = lax.all_gather(value, axis)]
  transfers between devices with their start and end apart: 17 -> 18, of which waited for: 7 -> 10; matrix products, arithmetic and copies ran while one was open for 7% -> 7% of each run, Pallas kernels for 0% -> 0%
where the time goes in v1:
time: 570 us; the launch traced here: 568 us
  waiting for transfers between devices  341 us (60%)
  blocking collectives  87.5 us (15%)
  starting transfers between devices  55.3 us (10%)
  matrix products  32.9 us (6%)
  between operations  24.5 us (4%)
  local copies, waits for them, and re-layouts  14.5 us (3%)
  other arithmetic  12.7 us (2%)
    psum x1, waiting for transfers between devices, shards(): lax.psum(lax.psum((grad_row_proj, grad_col_proj, jnp.stack([grad_row_pair...  199 us
    psum x1, waiting for transfers between devices, shards(): lax.psum((grad_row_proj, grad_col_proj, jnp.stack([grad_row_pair, grad_co...  79.8 us
    psum x1, blocking collectives, shards(): lax.psum(lax.psum((grad_row_proj, grad_col_proj, jnp.stack([grad_row_pair...  70.4 us
    all_gather x1, waiting for transfers between devices, total_of_pieces(): tiles = lax.all_gather(value, axis)  34 us
    all_to_all x3, starting transfers between devices, sent_to_all(): return lax.all_to_all(copies, axis, split_axis=0, concat_axis=0, tiled=True)  26.2 us
    psum x1, blocking collectives, shards(): lax.psum((grad_row_proj, grad_col_proj, jnp.stack([grad_row_pair, grad_co...  17.1 us
    ppermute x6, waiting for transfers between devices, padded_2(): after = lax.ppermute(leading, axis, down)  15.6 us
    ppermute x6, starting transfers between devices, padded_2(): after = lax.ppermute(leading, axis, down)  14.6 us
  transfers between devices with their start and end apart: 18, of which 10 were waited for; matrix products, arithmetic and copies ran while one was open for 7% of the time, Pallas kernels for 0%

profile of v1, /device:TPU:8, one launch (start us, length us, event | category | flops | bytes accessed | tf_op | source)
XLA Modules:
  0.0 568.3 jit_solution(14458506347573584178)
XLA Ops:
  7.2 1.0 convolution_convert_fusion.1
  8.8 6.3 %all-to-all-start = ((bf16[8,2,64]{2,1,0:T(2,128)(2,1)}), bf16[8,2,64]{2,1,0:T(2,128)(2,1)S(1)}, u32[]{:S(2)}, u32[]{:S(2)}) async-start(bf16[8,2,64]{2,1,0:T(2,128)(2,1)} %broadcast_in_dim.12), calls=%async_computation | async-start | bytes 8192 | tf_op jit(solution)/shard_map/all_to_all | solution.py:11
  15.1 1.1 fusion.201
  16.2 1.3 collective-permute-start.4
  17.6 1.3 collective-permute-start.5
  20.8 1.2 compare_and_fusion
  23.3 1.0 fusion.73
  25.0 0.7 reshape.293
  25.7 15.1 %all-to-all-start.1 = ((bf16[32,2,256]{2,1,0:T(2,128)(2,1)}), bf16[32,2,256]{2,1,0:T(2,128)(2,1)S(1)}, u32[]{:S(2)}, u32[]{:S(2)}) async-start(bf16[32,2,256]{2,1,0:T(2,128)(2,1)} %reshape.293), calls=%async_computation.1 | async-start | bytes 65536 | tf_op jit(solution)/shard_map/all_to_all | solution.py:11
  40.9 2.2 collective-permute-start
  43.1 1.3 collective-permute-start.1
  49.2 1.5 all-to-all-done.1
  51.0 3.3 collective-permute-start.2
  54.4 3.4 collective-permute-start.3
  57.8 0.8 convolution_bitcast_fusion.11
  58.7 1.3 collective-permute-done.3
  60.5 1.5 fusion.46
  62.6 4.3 collective-permute-start.6
  66.9 2.6 collective-permute-start.7
  69.5 4.6 multiply_convert_fusion
  74.2 6.0 %collective-permute-done.6 = bf16[64,32,8]{2,0,1:T(8,128)(2,1)S(1)} collective-permute-done((bf16[64,32,8]{2,0,1:T(8,128)(2,1)S(1)}, bf16[64,32,8]{2,0,1:T(8,128)(2,1)S(1)}, u32[]{:S(2)}, u32[]{:S(2)}) %collective-permute-start.6) | collective-permute-done | bytes 32800 | tf_op jit(solution)/shard_map/ppermute | solution.py:32
  80.2 9.6 %collective-permute-done.7 = bf16[64,32,8]{2,0,1:T(8,128)(2,1)S(1)} collective-permute-done((bf16[64,32,8]{2,0,1:T(8,128)(2,1)S(1)}, bf16[64,32,8]{2,0,1:T(8,128)(2,1)S(1)}, u32[]{:S(2)}, u32[]{:S(2)}) %collective-permute-start.7) | collective-permute-done | bytes 32800 | tf_op jit(solution)/shard_map/ppermute | solution.py:33
  89.8 1.1 pad_maximum_fusion
  93.7 1.8 fusion.208
  95.5 1.1 convolution_bitcast_fusion.7
  96.6 0.7 copy.231
  101.9 0.7 compare_and_fusion.3
  105.6 0.7 convolution_bitcast_fusion.12
  106.7 0.7 maximum_bitcast_fusion.4
  107.8 1.1 convolution_bitcast_fusion.15
  109.3 1.1 convolution_bitcast_fusion.16
  111.5 1.4 convolution_add_fusion.5
  112.9 0.7 convolution_bitcast_fusion.21
  113.7 0.8 reshape.295
  114.5 4.8 all-to-all-start.2
  119.4 0.7 pad_maximum_fusion.3
  120.1 4.3 all-to-all-done.2
  124.9 0.9 reduce
  126.3 1.3 collective-permute-start.8
  127.6 1.3 collective-permute-start.9
  129.6 2.8 collective-permute-done.9
  132.5 0.8 convolution_bitcast_fusion.10
  133.3 34.0 %all-gather.3.cloned.1.call-done = f32[96,256,64]{1,2,0:T(8,128)} async-done(((f32[3,256,64]{1,2,0:T(8,128)}), f32[96,256,64]{1,2,0:T(8,128)}) %all-gather.3.cloned.1.call-update) | async-done | bytes 6291472 | tf_op jit(solution)/shard_map/all_gather | solution.py:44
  167.3 3.2 reduce_sum.28
  170.9 2.1 collective-permute-start.10
  173.0 4.7 collective-permute-start.11
  178.0 0.9 pad_maximum_fusion.1
  178.9 1.9 collective-permute-done.11
  181.1 0.8 convolution_bitcast_fusion.9
  182.0 1.1 convolution_add_fusion.4
  183.1 1.1 convolution_add_fusion.3
  184.2 1.1 convolution_add_fusion.2
  185.3 79.8 %all-reduce.7.cloned.1.call-done = (f32[256,64]{0,1:T(8,128)}, f32[256,64]{0,1:T(8,128)}, f32[2,3,3,64,64]{3,4,1,2,0:T(8,128)}, f32[3,3,64,64]{3,2,1,0:T(8,128)}) async-done(((f32[256,64]{0,1:T(8,128)}, f32[256,64]{0,1:T(8,128)}, f32[2,3,3,64,64]{3,4,1,2,0:T(8,128)}, f32[3,3,64,64]{3,2,1,0:T(8,128)}), (f32[256,64]{0,1:T(8,128)}, f32[256,64]{0,1:T(8,128)}, f32[2,3,3,64,64]{3,4,1,2,0:T(8,128)}, ...) | async-done | bytes 573456 | tf_op jit(solution)/shard_map/psum | solution.py:276
  265.2 1.2 fusion.14
  266.4 1.1 copy.246
  267.5 17.1 %psum.76 = f32[64]{0:T(128)S(1)} all-reduce(f32[64]{0:T(128)S(1)} %copy-done.23), channel_id=1, replica_groups=mesh['row'=32,'col'=8] {'col'}, use_global_device_ids=true, to_apply=%region_9.10 | all-reduce | flops 64 | bytes 512 | tf_op jit(solution)/shard_map/psum | solution.py:276
  284.6 70.4 %psum.77 = f32[64]{0:T(128)} all-reduce(f32[64]{0:T(128)S(1)} %psum.76), channel_id=1, replica_groups=mesh['row'=32,'col'=8] {'row'}, use_global_device_ids=true, to_apply=%region_10.11 | all-reduce | flops 64 | bytes 512 | tf_op jit(solution)/shard_map/psum | solution.py:275
  355.0 0.7 fusion.178
  355.7 0.8 fusion.211
  356.5 199.4 %all-reduce.5.cloned.1.call-done = (f32[256,64]{0,1:T(8,128)}, f32[256,64]{0,1:T(8,128)}, f32[2,3,3,64,64]{3,4,1,2,0:T(8,128)}, f32[3,3,64,64]{3,2,1,0:T(8,128)}) async-done(((f32[256,64]{0,1:T(8,128)}, f32[256,64]{0,1:T(8,128)}, f32[2,3,3,64,64]{3,4,1,2,0:T(8,128)}, f32[3,3,64,64]{3,2,1,0:T(8,128)}), (f32[256,64]{0,1:T(8,128)}, f32[256,64]{0,1:T(8,128)}, f32[2,3,3,64,64]{3,4,1,2,0:T(8,128)}, ...) | async-done | bytes 573456 | tf_op jit(solution)/shard_map/psum | solution.py:275
  555.9 2.1 copy.247
  558.1 1.5 copy.333
  559.5 1.5 copy.334
  561.0 0.7 copy.335
  (134 shorter events, 16.5 us)
Async XLA Ops:
  7.2 17.1 %copy-start = (bf16[256,64]{0,1:T(8,128)(2,1)S(1)}, bf16[256,64]{0,1:T(8,128)(2,1)}, u32[]{:S(2)}) copy-start(bf16[256,64]{0,1:T(8,128)(2,1)} %param.12) | copy-start | bytes 98308
  7.2 16.1 %copy-start.1 = (bf16[64,16,256]{2,1,0:T(8,128)(2,1)S(1)}, bf16[64,16,256]{2,1,0:T(8,128)(2,1)}, u32[]{:S(2)}) copy-start(bf16[64,16,256]{2,1,0:T(8,128)(2,1)} %param.17) | copy-start | bytes 1572868
  7.2 11.7 %copy-start.17 = (s32[2]{0:T(128)S(1)}, s32[2]{0:T(128)}, u32[]{:S(2)}) copy-start(s32[2]{0:T(128)} %param.16) | copy-start | bytes 28
  7.2 16.0 %copy-start.3 = (bf16[2,3,3,64,64]{4,3,2,1,0:T(8,128)(2,1)S(1)}, bf16[2,3,3,64,64]{4,3,2,1,0:T(8,128)(2,1)}, u32[]{:S(2)}) copy-start(bf16[2,3,3,64,64]{4,3,2,1,0:T(8,128)(2,1)} %param.13) | copy-start | bytes 442372
  8.8 16.9 %all-to-all-start = ((bf16[8,2,64]{2,1,0:T(2,128)(2,1)}), bf16[8,2,64]{2,1,0:T(2,128)(2,1)S(1)}, u32[]{:S(2)}, u32[]{:S(2)}) async-start(bf16[8,2,64]{2,1,0:T(2,128)(2,1)} %broadcast_in_dim.12), calls=%async_computation | async-start | bytes 8192 | tf_op jit(solution)/shard_map/all_to_all | solution.py:11
  16.1 8.2 %copy-start.12 = (bf16[8,256]{1,0:T(8,128)(2,1)S(1)}, bf16[8,256]{1,0:T(8,128)(2,1)}, u32[]{:S(2)}) copy-start(bf16[8,256]{1,0:T(8,128)(2,1)} %param.10) | copy-start | bytes 12292
  16.2 45.8 %collective-permute-start.4 = (bf16[64,8,256]{2,0,1:T(8,128)(2,1)S(1)}, bf16[64,8,256]{2,0,1:T(8,128)(2,1)S(1)}, u32[]{:S(2)}, u32[]{:S(2)}) collective-permute-start(bf16[64,8,256]{2,0,1:T(8,128)(2,1)S(1)} %copy.319), channel_id=1, source_target_pairs={{0,8},{8,16},{16,24},{24,32},{32,40},{40,48},{48,56},{56,64},{64,7... | collective-permute-start | bytes 786440 | tf_op jit(solution)/shard_map/ppermute | solution.py:32
  17.6 44.7 %collective-permute-start.5 = (bf16[64,8,256]{2,0,1:T(8,128)(2,1)S(1)}, bf16[64,8,256]{2,0,1:T(8,128)(2,1)S(1)}, u32[]{:S(2)}, u32[]{:S(2)}) collective-permute-start(bf16[64,8,256]{2,0,1:T(8,128)(2,1)S(1)} %copy.320), channel_id=1, source_target_pairs={{8,0},{16,8},{24,16},{32,24},{40,32},{48,40},{56,48},{64,56},{72,6... | collective-permute-start | bytes 786440 | tf_op jit(solution)/shard_map/ppermute | solution.py:33
  25.7 25.0 %all-to-all-start.1 = ((bf16[32,2,256]{2,1,0:T(2,128)(2,1)}), bf16[32,2,256]{2,1,0:T(2,128)(2,1)S(1)}, u32[]{:S(2)}, u32[]{:S(2)}) async-start(bf16[32,2,256]{2,1,0:T(2,128)(2,1)} %reshape.293), calls=%async_computation.1 | async-start | bytes 65536 | tf_op jit(solution)/shard_map/all_to_all | solution.py:11
  40.9 126.5 %all-gather.3.cloned.1.call-start = ((), (), s32[]{:S(2)}) async-start(), calls=%async_computation.3 | async-start | bytes 6488064 | tf_op jit(solution)/shard_map/all_gather | solution.py:44
  40.9 8.2 %collective-permute-start = (bf16[16,64]{1,0:T(8,128)(2,1)S(1)}, bf16[16,64]{1,0:T(8,128)(2,1)S(1)}, u32[]{:S(2)}, u32[]{:S(2)}) collective-permute-start(bf16[16,64]{1,0:T(8,128)(2,1)S(1)} %bitcast.322), channel_id=1, source_target_pairs={{0,8},{8,16},{16,24},{24,32},{32,40},{40,48},{48,56},{56,64},{64,7... | collective-permute-start | bytes 6152 | tf_op jit(solution)/shard_map/ppermute | solution.py:32
  43.1 6.0 %collective-permute-start.1 = (bf16[16,64]{1,0:T(8,128)(2,1)S(1)}, bf16[16,64]{1,0:T(8,128)(2,1)S(1)}, u32[]{:S(2)}, u32[]{:S(2)}) collective-permute-start(bf16[16,64]{1,0:T(8,128)(2,1)S(1)} %bitcast.323), channel_id=1, source_target_pairs={{8,0},{16,8},{24,16},{32,24},{40,32},{48,40},{56,48},{64,56},{72,6... | collective-permute-start | bytes 6152 | tf_op jit(solution)/shard_map/ppermute | solution.py:33
  51.0 7.8 %collective-permute-start.2 = (bf16[16,64]{0,1:T(8,128)(2,1)S(1)}, bf16[16,64]{0,1:T(8,128)(2,1)S(1)}, u32[]{:S(2)}, u32[]{:S(2)}) collective-permute-start(bf16[16,64]{0,1:T(8,128)(2,1)S(1)} %copy.199), channel_id=1, source_target_pairs={{0,1},{1,2},{2,3},{3,4},{4,5},{5,6},{6,7},{8,9},{9,10},{10,11},{11... | collective-permute-start | bytes 6152 | tf_op jit(solution)/shard_map/ppermute | solution.py:32
  54.4 5.6 collective-permute-start.3
  62.2 7.3 %copy-start.18 = (pred[272,1]{0,1:T(4,128)(4,1)S(1)}, pred[272,1]{0,1:T(4,128)(4,1)}, u32[]{:S(2)}) copy-start(pred[272,1]{0,1:T(4,128)(4,1)} %get-tuple-element.93) | copy-start | bytes 820
  62.2 7.3 %copy-start.21 = (f32[64]{0:T(128)S(1)}, f32[64]{0:T(128)}, u32[]{:S(2)}) copy-start(f32[64]{0:T(128)} %param.14) | copy-start | bytes 772
  62.2 7.3 %copy-start.22 = (f32[3,32,64]{2,1,0:T(8,128)S(1)}, f32[3,32,64]{2,1,0:T(8,128)}, u32[]{:S(2)}) copy-start(f32[3,32,64]{2,1,0:T(8,128)} %convolution_bitcast_fusion.11) | copy-start | bytes 73732
  62.2 7.3 %copy-start.24 = (f32[32]{0:T(128)S(1)}, f32[32]{0:T(128)}, u32[]{:S(2)}) copy-start(f32[32]{0:T(128)} %and_convert_fusion) | copy-start | bytes 388
  62.6 17.7 %collective-permute-start.6 = (bf16[64,32,8]{2,0,1:T(8,128)(2,1)S(1)}, bf16[64,32,8]{2,0,1:T(8,128)(2,1)S(1)}, u32[]{:S(2)}, u32[]{:S(2)}) collective-permute-start(bf16[64,32,8]{2,0,1:T(8,128)(2,1)S(1)} %get-tuple-element.56), channel_id=1, source_target_pairs={{0,1},{1,2},{2,3},{3,4},{4,5},{5,6},{6,7},{8,9},{9,10},{10,11},{11... | collective-permute-start | bytes 98312 | tf_op jit(solution)/shard_map/ppermute | solution.py:32
  66.9 22.9 %collective-permute-start.7 = (bf16[64,32,8]{2,0,1:T(8,128)(2,1)S(1)}, bf16[64,32,8]{2,0,1:T(8,128)(2,1)S(1)}, u32[]{:S(2)}, u32[]{:S(2)}) collective-permute-start(bf16[64,32,8]{2,0,1:T(8,128)(2,1)S(1)} %get-tuple-element.57), channel_id=1, source_target_pairs={{1,0},{2,1},{3,2},{4,3},{5,4},{6,5},{7,6},{9,8},{10,9},{11,10},{12... | collective-permute-start | bytes 98312 | tf_op jit(solution)/shard_map/ppermute | solution.py:33
  74.2 16.7 %copy-start.4 = (bf16[3,3,64,64]{3,2,1,0:T(8,128)(2,1)S(1)}, bf16[3,3,64,64]{3,2,1,0:T(8,128)(2,1)}, u32[]{:S(2)}) copy-start(bf16[3,3,64,64]{3,2,1,0:T(8,128)(2,1)} %param.15) | copy-start | bytes 221188
  93.6 1.8 copy-start.20
  106.3 2.6 copy-start.5
  112.9 6.4 %copy-start.10 = (f32[1,64,64]{2,1,0:T(8,128)S(1)}, f32[1,64,64]{2,1,0:T(8,128)}, u32[]{:S(2)}) copy-start(f32[1,64,64]{2,1,0:T(8,128)} %convolution_bitcast_fusion.15) | copy-start | bytes 49156
  112.9 6.4 %copy-start.11 = (f32[1,64,64]{2,1,0:T(8,128)S(1)}, f32[1,64,64]{2,1,0:T(8,128)}, u32[]{:S(2)}) copy-start(f32[1,64,64]{2,1,0:T(8,128)} %convolution_bitcast_fusion.16) | copy-start | bytes 49156
  112.9 6.4 %copy-start.6 = (f32[1,3,64,64]{3,2,1,0:T(8,128)S(1)}, f32[1,3,64,64]{3,2,1,0:T(8,128)}, u32[]{:S(2)}) copy-start(f32[1,3,64,64]{3,2,1,0:T(8,128)} %maximum_bitcast_fusion.2) | copy-start | bytes 147460
  112.9 6.5 %copy-start.7 = (f32[1,3,64,64]{3,2,1,0:T(8,128)S(1)}, f32[1,3,64,64]{3,2,1,0:T(8,128)}, u32[]{:S(2)}) copy-start(f32[1,3,64,64]{3,2,1,0:T(8,128)} %maximum_bitcast_fusion.4) | copy-start | bytes 147460
  113.7 15.5 %copy-start.14 = (bf16[1,2,64]{2,1,0:T(2,128)(2,1)S(1)}, bf16[1,2,64]{2,1,0:T(2,128)(2,1)}, u32[]{:S(2)}) copy-start(bf16[1,2,64]{2,1,0:T(2,128)(2,1)} %get-tuple-element.80) | copy-start | bytes 772
  113.7 15.5 %copy-start.15 = (bf16[1,2,64]{2,1,0:T(2,128)(2,1)S(1)}, bf16[1,2,64]{2,1,0:T(2,128)(2,1)}, u32[]{:S(2)}) copy-start(bf16[1,2,64]{2,1,0:T(2,128)(2,1)} %get-tuple-element.81) | copy-start | bytes 772
  113.7 15.6 %copy-start.16 = (bf16[1,2,64]{2,1,0:T(2,128)(2,1)S(1)}, bf16[1,2,64]{2,1,0:T(2,128)(2,1)}, u32[]{:S(2)}) copy-start(bf16[1,2,64]{2,1,0:T(2,128)(2,1)} %get-tuple-element.82) | copy-start | bytes 772
  113.7 18.8 %copy-start.19 = (bf16[2,256]{1,0:T(2,128)(2,1)S(1)}, bf16[2,256]{1,0:T(2,128)(2,1)}, u32[]{:S(2)}) copy-start(bf16[2,256]{1,0:T(2,128)(2,1)} %param.9) | copy-start | bytes 3076
  114.5 9.9 %all-to-all-start.2 = ((f32[8,1,3072]{2,1,0:T(1,128)}), f32[8,1,3072]{2,1,0:T(1,128)S(1)}, u32[]{:S(2)}, u32[]{:S(2)}) async-start(f32[8,1,3072]{2,1,0:T(1,128)} %reshape.295), calls=%async_computation.2 | async-start | bytes 196608 | tf_op jit(solution)/shard_map/all_to_all | solution.py:11
  119.3 145.8 %all-reduce.7.cloned.1.call-start = ((), (), s32[]{:S(2)}) async-start(), calls=%async_computation.5 | async-start | bytes 2031616 | tf_op jit(solution)/shard_map/psum | solution.py:276
  126.3 3.3 collective-permute-start.8
  127.6 4.9 collective-permute-start.9
  170.9 10.2 %copy-start.13 = (bf16[8,256]{1,0:T(8,128)(2,1)S(1)}, bf16[8,256]{1,0:T(8,128)(2,1)}, u32[]{:S(2)}) copy-start(bf16[8,256]{1,0:T(8,128)(2,1)} %param.10) | copy-start | bytes 12292
  170.9 8.0 %collective-permute-start.10 = (f32[3,8,64]{1,2,0:T(8,128)S(1)}, f32[3,8,64]{1,2,0:T(8,128)S(1)}, u32[]{:S(2)}, u32[]{:S(2)}) collective-permute-start(f32[3,8,64]{1,2,0:T(8,128)S(1)} %get-tuple-element.65), channel_id=1, source_target_pairs={{0,1},{1,2},{2,3},{3,4},{4,5},{5,6},{6,7},{8,9},{9,10},{10,11},{11... | collective-permute-start | bytes 18440 | tf_op jit(solution)/shard_map/ppermute | solution.py:32
  173.0 7.8 %collective-permute-start.11 = (f32[3,8,64]{1,2,0:T(8,128)S(1)}, f32[3,8,64]{1,2,0:T(8,128)S(1)}, u32[]{:S(2)}, u32[]{:S(2)}) collective-permute-start(f32[3,8,64]{1,2,0:T(8,128)S(1)} %get-tuple-element.66), channel_id=1, source_target_pairs={{1,0},{2,1},{3,2},{4,3},{5,4},{6,5},{7,6},{9,8},{10,9},{11,10},{12... | collective-permute-start | bytes 18440 | tf_op jit(solution)/shard_map/ppermute | solution.py:33
  178.0 3.9 copy-start.2
  181.9 374.0 %all-reduce.5.cloned.1.call-start = ((), (), s32[]{:S(2)}) async-start(), calls=%async_computation.4 | async-start | bytes 2031616 | tf_op jit(solution)/shard_map/psum | solution.py:275
  265.2 2.3 copy-start.23
  265.2 89.8 %copy-start.9 = (bf16[256,64]{0,1:T(8,128)(2,1)S(1)}, bf16[256,64]{0,1:T(8,128)(2,1)}, u32[]{:S(2)}) copy-start(bf16[256,64]{0,1:T(8,128)(2,1)} %param.11) | copy-start | bytes 98308
  555.9 5.1 copy-start.8
Sparse Core Ops, SparseCore 0:
  97.4 69.8 all-gather.2
  182.0 83.0 all-reduce.6
  268.0 287.8 all-reduce.4
